TPU v7x, 32 devices: a whole 2x2x4 slice. The times are simulated.
32 devices in a mesh: ctx: 8 (over z, y), head: 4 (over x, core).
Axes of the slice: x: 2, y: 2, z: 4, core: 2. Of those that a mesh axis runs over, the one named last changes fastest.
Arguments:
- queries: bfloat16 [2048, 4096], P('ctx', 'head'), may hold values from -48 to 48
- enc_keys: bfloat16 [256, 4096], P('ctx', 'head'), may hold values from -4 to 4
- enc_values: bfloat16 [256, 4096], P('ctx', 'head'), may hold values from -6 to 6
- grad_out: bfloat16 [2048, 4096], P('ctx', 'head'), may hold values from -48 to 48
- out_weight: bfloat16 [4096, 4096], P('head'), may hold values from -0.09375 to 0.09375
Outputs:
- query_grad: bfloat16 [2048, 4096], P('ctx', 'head')
- key_grad: bfloat16 [256, 4096], P('ctx', 'head')
- value_grad: bfloat16 [256, 4096], P('ctx', 'head')
All inputs are finite; a program needn't handle non-finite values.
Results may differ from a plain program's by a relative error of at most 0.0085.
Values may be sent and summed in bfloat16 or wider, within the bound.
A program may use at most 64 MiB of HBM per device.

v0:
```python
from functools import partial
import math

import jax
import jax.numpy as jnp
from jax import lax
from jax.sharding import PartitionSpec as P

DH = 64


def run_blocks(step_fn, running, arrays, block_rows):
    block_count = arrays[0].shape[0] // block_rows
    blocked = tuple((block.reshape(block_count, block_rows, block.shape[1]) for block in arrays))

    def scan_step(current, scanned):
        position, pieces = scanned
        return (step_fn(current, pieces, position * block_rows), None)

    running, _ = lax.scan(scan_step, running, (jnp.arange(block_count, dtype=jnp.int32), blocked))
    return running


def local(queries, enc_keys, enc_values, grad_out, out_weight):
    query_rows, head_width = queries.shape
    heads_here = head_width // DH
    score_scale = DH ** (-0.5)
    head_grads = lax.dot_general(
        lax.all_gather(grad_out, "head", axis=1, tiled=True),
        out_weight,
        (((1,), (1,)), ((), ())),
        preferred_element_type=jnp.float32,
    ).astype(jnp.bfloat16)
    query_heads = queries.reshape(query_rows, heads_here, DH)
    grad_heads = head_grads.reshape(query_rows, heads_here, DH)

    def block_scores(key_block):
        key_count = key_block.shape[0]
        return score_scale * jnp.einsum(
            "qhd,khd->hqk",
            query_heads,
            key_block.reshape(key_count, heads_here, DH),
            preferred_element_type=jnp.float32,
        )

    def stats_step(current, pieces, offset):
        row_top, row_total = current
        scores = block_scores(pieces[0])
        new_top = jnp.maximum(row_top, jnp.max(scores, axis=2))
        exponent = jnp.exp(scores - new_top[:, :, None])
        return (new_top, row_total * jnp.exp(row_top - new_top) + jnp.sum(exponent, axis=2))

    def block_attention(row_stats, pieces):
        scores = block_scores(pieces[0])
        return jnp.exp(scores - row_stats[0][:, :, None]) / row_stats[1][:, :, None]

    def output_step(row_stats, current, pieces, offset):
        attention_low = block_attention(row_stats, pieces).astype(jnp.bfloat16)
        value_block = pieces[1].reshape(pieces[1].shape[0], heads_here, DH)
        return current + jnp.einsum(
            "hqk,khd->qhd", attention_low, value_block, preferred_element_type=jnp.float32
        )

    def score_grads(row_stats, row_delta, pieces):
        attention = block_attention(row_stats, pieces)
        value_block = pieces[1].reshape(pieces[1].shape[0], heads_here, DH)
        prob_grad = jnp.einsum(
            "qhd,khd->hqk", grad_heads, value_block, preferred_element_type=jnp.float32
        )
        score_grad = (score_scale * attention * (prob_grad - row_delta[:, :, None])).astype(
            jnp.bfloat16
        )
        return (attention.astype(jnp.bfloat16), score_grad)

    def query_term(score_grad, key_block):
        key_heads = key_block.reshape(key_block.shape[0], heads_here, DH)
        return jnp.einsum("hqk,khd->qhd", score_grad, key_heads, preferred_element_type=jnp.float32)

    def query_step(row_stats, row_delta, current, pieces, offset):
        attention_low, score_grad = score_grads(row_stats, row_delta, pieces)
        return current + query_term(score_grad, pieces[0])

    stats_start = (
        jnp.full((heads_here, query_rows), -1e30, jnp.float32),
        jnp.zeros((heads_here, query_rows), jnp.float32),
    )
    attended_start = jnp.zeros((query_rows, heads_here, DH), jnp.float32)
    total_keys = enc_keys.shape[0] * lax.axis_size("ctx")
    all_keys, all_values = (
        lax.all_gather(enc_keys, "ctx", axis=0, tiled=True),
        lax.all_gather(enc_values, "ctx", axis=0, tiled=True),
    )
    block_rows = math.gcd(total_keys, 512)
    row_stats = run_blocks(stats_step, stats_start, (all_keys,), block_rows)
    attended = run_blocks(
        partial(output_step, row_stats), attended_start, (all_keys, all_values), block_rows
    )
    row_delta = jnp.einsum("qhd,qhd->hq", grad_heads.astype(jnp.float32), attended)
    query_sum = run_blocks(
        partial(query_step, row_stats, row_delta),
        attended_start,
        (all_keys, all_values),
        block_rows,
    )
    pieces = (all_keys, all_values)
    attention_low, score_grad = score_grads(row_stats, row_delta, pieces)
    key_count = lax.axis_size("ctx") * enc_keys.shape[0]
    key_term = jnp.einsum(
        "hqk,qhd->khd", score_grad, query_heads, preferred_element_type=jnp.float32
    )
    value_term = jnp.einsum(
        "hqk,qhd->khd", attention_low, grad_heads, preferred_element_type=jnp.float32
    )
    key_term, value_term = (
        key_term.reshape(key_count, head_width),
        value_term.reshape(key_count, head_width),
    )
    stacked = lax.psum_scatter(
        jnp.concatenate((key_term, value_term), axis=1), "ctx", scatter_dimension=0, tiled=True
    )
    key_grad = stacked[:, :head_width]
    value_grad = stacked[:, head_width:]
    query_grad = query_sum.reshape(query_rows, head_width).astype(jnp.bfloat16)
    return (query_grad, key_grad.astype(jnp.bfloat16), value_grad.astype(jnp.bfloat16))


def solution(mesh):
    return jax.shard_map(
        local,
        mesh=mesh,
        in_specs=(
            P("ctx", "head"),
            P("ctx", "head"),
            P("ctx", "head"),
            P("ctx", "head"),
            P("head", None),
        ),
        out_specs=(P("ctx", "head"), P("ctx", "head"), P("ctx", "head")),
        check_vma=False,
    )
```

profile of v0, /device:TPU:0, one launch (start us, length us, event | category | flops | bytes accessed | tf_op | source)
XLA Modules:
  0.0 182.4 jit_solution(8599344071962932298)
XLA Ops:
  7.2 0.0 all-gather.2.cloned.1.call-start
  7.2 0.7 all-gather.2.cloned.1.call-update
  7.9 0.0 reduce-scatter.2.cloned.1.call-start
  7.9 33.2 %all_gather.9 = bf16[256,1024]{1,0:T(8,128)(2,1)S(1)} all-gather(bf16[32,1024]{1,0:T(8,128)(2,1)} %param.6), channel_id=1, replica_groups=mesh['ctx'=8,'head'=4] {'ctx'}, dimensions={0}, use_global_device_ids=true | all-gather | bytes 589824 | tf_op jit(solution)/shard_map/all_gather | solution.py:90
  41.2 0.2 copy.22
  41.4 31.5 %all_gather.11 = bf16[256,1024]{1,0:T(8,128)(2,1)S(1)} all-gather(bf16[32,1024]{1,0:T(8,128)(2,1)} %param.7), channel_id=1, replica_groups=mesh['ctx'=8,'head'=4] {'ctx'}, dimensions={0}, use_global_device_ids=true | all-gather | bytes 589824 | tf_op jit(solution)/shard_map/all_gather | solution.py:91
  72.9 1.0 copy.24
  73.9 1.2 copy.21
  75.1 0.8 multiply_reduce_fusion
  75.9 0.0 copy-start
  75.9 1.9 %copy-done = f32[16,256,256]{1,2,0:T(8,128)} copy-done((f32[16,256,256]{1,2,0:T(8,128)}, f32[16,256,256]{1,2,0:T(8,128)S(1)}, u32[]{:S(2)}) %copy-start) | copy-done | bytes 4194328
  77.8 0.7 fusion.1
  78.6 0.0 all-gather.2.cloned.1.call-done
  78.6 6.4 %convolution_convert_fusion = bf16[256,1024]{1,0:T(8,128)(2,1)S(1)} fusion(bf16[256,4096]{1,0:T(8,128)(2,1)} %all-gather.2.cloned.1.call-done, bf16[1024,4096]{1,0:T(8,128)(2,1)} %param.9), kind=kOutput, calls=%fused_computation.7 | convolution fusion | flops 2147745792 | bytes 11010048 | tf_op jit(solution)/shard_map/dot_general | solution.py:28
  85.0 1.0 copy.23
  86.0 1.4 copy.38
  87.4 0.0 copy-start.1
  87.4 0.0 copy-start.3
  87.4 4.4 %fusion.2 = f32[16,64,256]{2,1,0:T(8,128)} fusion(bf16[256,16,64]{0,2,1:T(8,128)(2,1)} %bitcast.37, f32[16,256,256]{1,2,0:T(8,128)} %copy-done, f32[16,256]{1,0:T(8,128)S(1)} %multiply_add_fusion, f32[16,256]{1,0:T(8,128)S(1)} %broadcast_maximum_fusion), kind=kOutput, calls=%fused_computation.9 | convolution fusion | flops 138412032 | bytes 5799936 | tf_op jit(solution)/shard_map/hqk,qhd->khd/dot_general | solution.py:111
  91.8 0.0 copy-done.1
  91.9 1.6 multiply_reduce_fusion.1
  93.4 1.5 multiply_convert_fusion
  94.9 2.6 %copy.30 = f32[256,1024]{1,0:T(8,128)} copy(f32[256,1024]{0,1:T(8,128)} %bitcast.40) | data formatting | bytes 2097152 | tf_op jit(solution)/shard_map/reshape | solution.py:116
  97.5 1.7 fusion.8
  99.2 2.5 %copy.29 = f32[256,1024]{1,0:T(8,128)} copy(f32[256,1024]{0,1:T(8,128)} %bitcast.35) | data formatting | bytes 2097152 | tf_op jit(solution)/shard_map/reshape | solution.py:115
  101.8 3.1 %pad_maximum_fusion = f32[256,2048]{1,0:T(8,128)} fusion(f32[256,1024]{1,0:T(8,128)} %copy.30, f32[256,1024]{1,0:T(8,128)} %copy.29), kind=kLoop, calls=%fused_computation.5 | loop fusion | flops 524288 | bytes 4194304 | tf_op jit(solution)/shard_map/concatenate | solution.py:119
  104.9 0.0 reduce-scatter.2.cloned.1.call-update
  104.9 0.5 convolution_convert_fusion.1
  105.4 1.0 copy.31
  106.4 67.5 %reduce-scatter.2.cloned.1.call-done = f32[32,2048]{1,0:T(8,128)} async-done(((f32[256,2048]{1,0:T(8,128)}), f32[32,2048]{1,0:T(8,128)}) %reduce-scatter.2.cloned.1.call-update) | async-done | bytes 262160 | tf_op jit(solution)/shard_map/reduce_scatter | solution.py:118
  173.9 1.0 convert.4
  174.9 0.7 fusion.7
  (5 shorter events, 0.0 us)
Async XLA Ops:
  7.2 71.4 %all-gather.2.cloned.1.call-start = ((), (), s32[]{:S(2)}) async-start(), calls=%async_computation.1 | async-start | bytes 2621440 | tf_op jit(solution)/shard_map/all_gather | solution.py:29
  7.9 166.0 %reduce-scatter.2.cloned.1.call-start = ((), (), s32[]{:S(2)}) async-start(), calls=%async_computation.2 | async-start | bytes 2359296 | tf_op jit(solution)/shard_map/reduce_scatter | solution.py:118
  75.9 1.9 %copy-start = (f32[16,256,256]{1,2,0:T(8,128)}, f32[16,256,256]{1,2,0:T(8,128)S(1)}, u32[]{:S(2)}) copy-start(f32[16,256,256]{1,2,0:T(8,128)S(1)} %get-tuple-element.66) | copy-start | bytes 12582916
  87.4 4.5 %copy-start.1 = (f32[16,256,256]{1,2,0:T(8,128)S(1)}, f32[16,256,256]{1,2,0:T(8,128)}, u32[]{:S(2)}) copy-start(f32[16,256,256]{1,2,0:T(8,128)} %copy-done) | copy-start | bytes 12582916
  87.4 4.5 %copy-start.3 = (bf16[256,1024]{0,1:T(8,128)(2,1)S(1)}, bf16[256,1024]{0,1:T(8,128)(2,1)}, u32[]{:S(2)}) copy-start(bf16[256,1024]{0,1:T(8,128)(2,1)} %copy.24) | copy-start | bytes 1572868
  91.8 1.6 copy-start.2
Sparse Core Ops, SparseCore 0:
  9.6 25.2 all-gather.1
  105.0 68.8 reduce-scatter.1
where the time goes:
time: 183 us; the launch traced here: 182 us
  waiting for transfers between devices  68.3 us (37%)
  blocking collectives  64.7 us (35%)
  matrix products  16.8 us (9%)
  between operations  14.2 us (8%)
  local copies, waits for them, and re-layouts  13.5 us (7%)
  other arithmetic  4.8 us (3%)
    reduce_scatter x1, waiting for transfers between devices, local(): lax.psum_scatter(jnp.concatenate((key_term, value_term), axis=1), 'ctx',...  67.5 us
    all_gather x1, blocking collectives, local(): lax.all_gather(enc_keys, 'ctx', axis=0, tiled=True)  33.2 us
    all_gather x1, blocking collectives, local(): lax.all_gather(enc_values, 'ctx', axis=0, tiled=True)  31.5 us
    dot_general x1, matrix products, local(): lax.dot_general(lax.all_gather(grad_out, 'head', axis=1, tiled=True), out...  6.38 us
    unnamed x11, local copies, waits for them, and re-layouts  5.56 us
    dot_general x1, matrix products, local(): jnp.einsum('hqk,qhd->khd', attention_low, grad_heads, preferred_element_t...  4.45 us
  transfers between devices with their start and end apart: 2, of which 1 were waited for; matrix products, arithmetic and copies ran while one was open for 3% of the time, Pallas kernels for 0%

commit v1 on v0

v1 whole, which is shorter than its diff:
```python
import functools

import jax
import jax.numpy as jnp
from jax import lax
from jax.experimental import pallas as pl
from jax.experimental.pallas import tpu as pltpu
from jax.sharding import PartitionSpec as P

DH = 64
PAIR = 2 * DH
MESH = pl.DeviceIdType.MESH
NT = (((1,), (1,)), ((), ()))
NN = (((1,), (0,)), ((), ()))


def dot(a, b, dims):
    return lax.dot_general(a, b, dims, preferred_element_type=jnp.float32)


def inner_extent(n):
    best = 1
    while n % (2 * best) == 0 and (2 * best) ** 2 <= n:
        best *= 2
    return best


def kernel(Z, Y, X, C, kc, q_hbm, k_hbm, v_hbm, g_hbm, w_hbm, dq_ref, dk_ref, dv_ref,
           qbuf, q2buf, kvbuf, ktbuf, gbuf, wbuf, acc, dobuf, pbuf, dsbuf, part, s1, r1, s2, r2,
           loc_sem, w_sem, g_recv, gx_send, gc_send, gf_send, kv_recv, kvz_send, kvy_send, kvf_send,
           s1_send, r1_recv, s2_send, r2_recv):
    rows, width = q_hbm.shape
    r = k_hbm.shape[0]
    keys = Z * Y * r
    half = Z * r
    pairs = width // PAIR
    chunks = width // kc
    c = lax.axis_index("ctx")
    h = lax.axis_index("head")
    z, y = c // Y, c % Y
    x, k = h // C, h % C

    def at_z(b):
        return {"ctx": lax.rem(z + b, Z) * Y + y, "head": h}

    def at_y(a):
        return {"ctx": z * Y + lax.rem(y + a, Y), "head": h}

    def at_x(d):
        return {"ctx": c, "head": lax.rem(x + d, X) * C + k}

    def at_core(d):
        return {"ctx": c, "head": x * C + lax.rem(k + d, C)}

    def remote(src, dst, send, recv, target):
        return pltpu.make_async_remote_copy(
            src_ref=src, dst_ref=dst, send_sem=send, recv_sem=recv,
            device_id=target, device_id_type=MESH)

    def slot(a, b):
        return pl.ds((a * Z + b) * r, r)

    kv_hbm = (k_hbm, v_hbm)

    loads = [
        pltpu.make_async_copy(g_hbm, gbuf.at[0, 0], loc_sem.at[0]),
        pltpu.make_async_copy(q_hbm, qbuf, loc_sem.at[1]),
        pltpu.make_async_copy(k_hbm, kvbuf.at[0, slot(0, 0)], loc_sem.at[2]),
        pltpu.make_async_copy(v_hbm, kvbuf.at[1, slot(0, 0)], loc_sem.at[3]),
    ]

    def w_load(d, e):
        block = lax.rem(x + d, X) * C + lax.rem(k + e, C)
        cols = pl.ds(pl.multiple_of(block * width, width), width)
        return pltpu.make_async_copy(w_hbm.at[:, cols], wbuf.at[d, e], w_sem.at[d, e])

    loads[0].start()
    w_load(0, 0).start()
    for copy in loads[1:]:
        copy.start()
    for d in range(X):
        for e in range(C):
            if d + e:
                w_load(d, e).start()

    partners = ([at_z(b) for b in range(1, Z)] + [at_y(a) for a in range(1, Y)]
                + [at_x(d) for d in range(1, X)] + [at_core(d) for d in range(1, C)])
    barrier = pltpu.get_barrier_semaphore()
    for target in partners:
        pl.semaphore_signal(barrier, inc=1, device_id=target, device_id_type=MESH)
    pl.semaphore_wait(barrier, len(partners))

    def cols(j):
        return pl.ds(j * kc, kc)

    def gx(d, j):
        return remote(g_hbm.at[:, cols(j)], gbuf.at[X - d, 0, :, cols(j)],
                      gx_send.at[d, j], g_recv.at[X - d, 0, j], at_x(d))

    def gc(e):
        return remote(g_hbm, gbuf.at[0, C - e], gc_send.at[e], g_recv.at[0, C - e, 0], at_core(e))

    def gf(d, e, j):
        return remote(gbuf.at[d, 0, :, cols(j)], gbuf.at[d, C - e, :, cols(j)],
                      gf_send.at[d, e, j], g_recv.at[d, C - e, j], at_core(e))

    def kvz(t, b):
        return remote(kv_hbm[t], kvbuf.at[t, slot(0, Z - b)],
                      kvz_send.at[t, b], kv_recv.at[t, 0, Z - b], at_z(b))

    def kvy(t, a):
        return remote(kv_hbm[t], kvbuf.at[t, slot(Y - a, 0)],
                      kvy_send.at[t, a], kv_recv.at[t, Y - a, 0], at_y(a))

    def kvf(t, a, b):
        return remote(kvbuf.at[t, slot(0, b)], kvbuf.at[t, slot(Y - a, b)],
                      kvf_send.at[t, a, b], kv_recv.at[t, Y - a, b], at_y(a))

    for d in range(1, X):
        gx(d, 0).start()
    for t in range(2):
        for b in range(1, Z):
            kvz(t, b).start()
        for a in range(1, Y):
            kvy(t, a).start()
    for j in range(1, chunks):
        for d in range(1, X):
            gx(d, j).start()
    for e in range(1, C):
        gc(e).start()

    def forward_g(j):
        for d in range(1, X):
            gx(X - d, j).wait_recv()
            for e in range(1, C):
                gf(d, e, j).start()

    def forward_kv(t):
        for b in range(1, Z):
            kvz(t, Z - b).wait_recv()
            for a in range(1, Y):
                kvf(t, a, b).start()

    def arrived_kv(t):
        for a in range(1, Y):
            kvy(t, Y - a).wait_recv()
            for b in range(1, Z):
                kvf(t, Y - a, b).wait_recv()

    def add_chunk(j):
        total = acc[...]
        for d in range(1, X):
            for e in range(C):
                if e:
                    gf(d, C - e, j).wait_recv()
                total += dot(gbuf[d, e, :, j * kc:(j + 1) * kc], wbuf[d, e, :, j * kc:(j + 1) * kc], NT)
        acc[...] = total

    loads[0].wait()
    w_load(0, 0).wait()
    acc[...] = dot(gbuf[0, 0], wbuf[0, 0], NT)
    for e in range(1, C):
        gc(C - e).wait_recv()
        w_load(0, e).wait()
        acc[...] += dot(gbuf[0, e], wbuf[0, e], NT)
    for d in range(1, X):
        for e in range(C):
            w_load(d, e).wait()

    lane = lax.broadcasted_iota(jnp.int32, (1, PAIR), 1)
    low = jnp.where(lane < DH, 1.0, 0.0).astype(jnp.bfloat16)
    high = jnp.where(lane < DH, 0.0, 1.0).astype(jnp.bfloat16)
    scale = DH ** -0.5

    def at_pair(p):
        return pl.ds(pl.multiple_of(p * PAIR, PAIR), PAIR)

    def both_heads(block):
        return jnp.concatenate((block * low, block * high), axis=0)

    def attention(p, carry):
        q2 = both_heads(qbuf[:, at_pair(p)] * jnp.bfloat16(scale))
        q2buf[p] = q2
        key_pair = kvbuf[0, :, at_pair(p)]
        ktbuf[p] = key_pair.astype(jnp.float32).T.astype(jnp.bfloat16)
        scores = dot(key_pair, q2, NT)
        exponent = jnp.exp(scores - jnp.max(scores, axis=0, keepdims=True))
        pbuf[p] = exponent * (1.0 / jnp.sum(exponent, axis=0, keepdims=True))
        return carry

    loads[1].wait()
    loads[2].wait()
    forward_g(0)
    forward_kv(0)
    done = 0
    for j in range(1, chunks):
        if j == 1:
            arrived_kv(0)
        forward_g(j)
        if j == min(2, chunks - 1):
            forward_kv(1)
        add_chunk(j - 1)
        upto = pairs * j // (chunks - 1)
        lax.fori_loop(done, upto, attention, 0)
        done = upto
    if chunks == 1:
        arrived_kv(0)
        forward_kv(1)
        lax.fori_loop(0, pairs, attention, 0)
    add_chunk(chunks - 1)
    dobuf[...] = acc[...].astype(jnp.bfloat16)
    loads[3].wait()
    arrived_kv(1)

    def send1(a, p):
        return remote(s1.at[a - 1, p], r1.at[Y - a - 1, p], s1_send.at[a - 1, p],
                      r1_recv.at[Y - a - 1, p], at_y(a))

    def send2(b, p):
        return remote(s2.at[b - 1, p], r2.at[Z - b - 1, p], s2_send.at[b - 1, p],
                      r2_recv.at[Z - b - 1, p], at_z(b))

    def terms(p):
        do2 = both_heads(dobuf[:, at_pair(p)])
        prob = pbuf[p]
        prob_low = prob.astype(jnp.bfloat16)
        dp = dot(kvbuf[1, :, at_pair(p)], do2, NT)
        delta = jnp.sum(prob_low.astype(jnp.float32) * dp, axis=0, keepdims=True)
        ds = (prob * (dp - delta)).astype(jnp.bfloat16)
        dsbuf[p] = ds
        for t, term in enumerate((dot(ds, q2buf[p], NN), dot(prob_low, do2, NN))):
            part[p, t] = term[:half]
            for a in range(1, Y):
                s1[a - 1, p, t] = term[a * half:(a + 1) * half].astype(jnp.bfloat16)
        for a in range(1, Y):
            send1(a, p).start()

    def second(p):
        for a in range(1, Y):
            send1(Y - a, p).wait_recv()
        for t in range(2):
            total = part[p, t]
            for a in range(1, Y):
                total += r1[a - 1, p, t].astype(jnp.float32)
            part[p, t, :r] = total[:r]
            for b in range(1, Z):
                s2[b - 1, p, t] = total[b * r:(b + 1) * r].astype(jnp.bfloat16)
        for b in range(1, Z):
            send2(b, p).start()

    def query_part(p):
        dqt = dot(ktbuf[p], dsbuf[p], NN)
        both = jnp.concatenate((dqt[:DH, :rows], dqt[DH:, rows:]), axis=0)
        dq_ref[:, at_pair(p)] = (both.T * scale).astype(jnp.bfloat16)

    lag = min(2, pairs)

    def first_loop(p, carry):
        terms(p)

        @pl.when(p >= lag)
        def _():
            second(p - lag)
        return carry

    lax.fori_loop(0, pairs, first_loop, 0)

    def tail_loop(p, carry):
        query_part(p)

        @pl.when(p >= pairs - lag)
        def _():
            second(p)
        return carry

    lax.fori_loop(0, pairs, tail_loop, 0)

    def final_loop(p, carry):
        for b in range(1, Z):
            send2(Z - b, p).wait_recv()
        for t, out in enumerate((dk_ref, dv_ref)):
            total = part[p, t, :r]
            for b in range(1, Z):
                total += r2[b - 1, p, t].astype(jnp.float32)
            out[:, at_pair(p)] = total.astype(jnp.bfloat16)
        for a in range(1, Y):
            send1(a, p).wait_send()
        for b in range(1, Z):
            send2(b, p).wait_send()
        return carry

    lax.fori_loop(0, pairs, final_loop, 0)

    for j in range(chunks):
        for d in range(1, X):
            gx(d, j).wait_send()
            for e in range(1, C):
                gf(d, e, j).wait_send()
    for e in range(1, C):
        gc(e).wait_send()
    for t in range(2):
        for b in range(1, Z):
            kvz(t, b).wait_send()
            for a in range(1, Y):
                kvf(t, a, b).wait_send()
        for a in range(1, Y):
            kvy(t, a).wait_send()


def local(n, m, queries, enc_keys, enc_values, grad_out, out_weight):
    rows, width = queries.shape
    r = enc_keys.shape[0]
    Y = inner_extent(n)
    Z = n // Y
    C = 2 if m % 2 == 0 else 1
    X = m // C
    kc = min(256, width)
    pairs = width // PAIR
    chunks = width // kc
    keys, half = n * r, Z * r
    low, full = jnp.bfloat16, jnp.float32
    y1, z1 = max(Y - 1, 1), max(Z - 1, 1)
    dma = pltpu.SemaphoreType.DMA
    vmem = pltpu.VMEM
    return pl.pallas_call(
        functools.partial(kernel, Z, Y, X, C, kc),
        out_shape=(
            jax.ShapeDtypeStruct((rows, width), low),
            jax.ShapeDtypeStruct((r, width), low),
            jax.ShapeDtypeStruct((r, width), low),
        ),
        in_specs=[pl.BlockSpec(memory_space=pl.ANY)] * 5,
        out_specs=[pl.BlockSpec(memory_space=pltpu.VMEM)] * 3,
        scratch_shapes=[
            vmem((rows, width), low),
            vmem((pairs, 2 * rows, PAIR), low),
            vmem((2, keys, width), low),
            vmem((pairs, PAIR, keys), low),
            vmem((X, C, rows, width), low),
            vmem((X, C, width, width), low),
            vmem((rows, width), full),
            vmem((rows, width), low),
            vmem((pairs, keys, 2 * rows), full),
            vmem((pairs, keys, 2 * rows), low),
            vmem((pairs, 2, half, PAIR), full),
            vmem((y1, pairs, 2, half, PAIR), low),
            vmem((y1, pairs, 2, half, PAIR), low),
            vmem((z1, pairs, 2, r, PAIR), low),
            vmem((z1, pairs, 2, r, PAIR), low),
            dma((4,)),
            dma((X, C)),
            dma((X, C, chunks)),
            dma((X, chunks)),
            dma((C,)),
            dma((X, C, chunks)),
            dma((2, Y, Z)),
            dma((2, Z)),
            dma((2, Y)),
            dma((2, Y, Z)),
            dma((y1, pairs)),
            dma((y1, pairs)),
            dma((z1, pairs)),
            dma((z1, pairs)),
        ],
        compiler_params=pltpu.CompilerParams(
            collective_id=0, has_side_effects=True, vmem_limit_bytes=52 * 1024 * 1024),
    )(queries, enc_keys, enc_values, grad_out, out_weight)


def solution(mesh):
    return jax.shard_map(
        functools.partial(local, mesh.shape["ctx"], mesh.shape["head"]),
        mesh=mesh,
        in_specs=(
            P("ctx", "head"),
            P("ctx", "head"),
            P("ctx", "head"),
            P("ctx", "head"),
            P("head", None),
        ),
        out_specs=(P("ctx", "head"), P("ctx", "head"), P("ctx", "head")),
        check_vma=False,
    )
```

time: 183 us -> 53.8 us (0.29)
  waiting for transfers between devices: 68.3 us -> 0 us
  blocking collectives: 64.7 us -> 0 us
  Pallas kernels: 0 us -> 47 us
  matrix products: 16.8 us -> 0 us
  between operations: 14.2 us -> 0.65 us
  local copies, waits for them, and re-layouts: 13.5 us -> 5.81 us
  other arithmetic: 4.8 us -> 0 us
    reduce_scatter x1 -> x0, waiting for transfers between devices: 67.5 us -> none  [local(): lax.psum_scatter(jnp.concatenate((key_term, value_term), axis=1), 'ctx',...]
    all_gather x2 -> x0, blocking collectives: 64.7 us -> none  [the longest x1 33.2 us: local(): lax.all_gather(enc_keys, 'ctx', axis=0, tiled=True)]
    pallas_call x0 -> x1, Pallas kernels: none -> 47 us  [local(): pl.pallas_call(functools.partial(kernel, Z, Y, X, C, kc), out_shape=(jax....]
    dot_general x7 -> x0, matrix products: 16.8 us -> none  [the longest x1 6.38 us: local(): lax.dot_general(lax.all_gather(grad_out, 'head', axis=1, tiled=True), out...]
    reshape x2 -> x0, local copies, waits for them, and re-layouts: 5.1 us -> none  [the longest x1 2.56 us: local(): value_term.reshape(key_count, head_width)]
    concatenate x1 -> x0, other arithmetic: 3.11 us -> none  [local(): jnp.concatenate((key_term, value_term), axis=1)]
  transfers between devices with their start and end apart: 2 -> 0, of which waited for: 1 -> 0; matrix products, arithmetic and copies ran while one was open for 3% -> 0% of each run, Pallas kernels for 0% -> 0%
where the time goes in v1:
time: 53.8 us; the launch traced here: 53.5 us
  Pallas kernels  47 us (87%)
  local copies, waits for them, and re-layouts  5.81 us (11%)
  between operations  0.65 us (1%)
    pallas_call x1, Pallas kernels, local(): pl.pallas_call(functools.partial(kernel, Z, Y, X, C, kc), out_shape=(jax....  47 us
    unnamed x11, local copies, waits for them, and re-layouts  5.81 us

profile of v1, /device:TPU:0, one launch (start us, length us, event | category | flops | bytes accessed | tf_op | source)
XLA Modules:
  0.0 53.5 jit_solution(3747252682193912669)
XLA Ops:
  0.6 0.0 copy-start
  0.6 1.0 %copy-done = bf16[256,1024]{1,0:T(8,128)(2,1)S(1)} copy-done((bf16[256,1024]{1,0:T(8,128)(2,1)S(1)}, bf16[256,1024]{1,0:T(8,128)(2,1)}, u32[]{:S(2)}) %copy-start) | copy-done | bytes 524312
  1.7 0.0 copy-start.1
  1.7 1.0 %copy-done.1 = bf16[256,1024]{1,0:T(8,128)(2,1)S(1)} copy-done((bf16[256,1024]{1,0:T(8,128)(2,1)S(1)}, bf16[256,1024]{1,0:T(8,128)(2,1)}, u32[]{:S(2)}) %copy-start.1) | copy-done | bytes 524312
  2.7 0.0 copy-start.2
  2.7 0.8 %copy-done.2 = bf16[32,1024]{1,0:T(8,128)(2,1)S(1)} copy-done((bf16[32,1024]{1,0:T(8,128)(2,1)S(1)}, bf16[32,1024]{1,0:T(8,128)(2,1)}, u32[]{:S(2)}) %copy-start.2) | copy-done | bytes 65560
  3.6 0.0 copy-start.3
  3.6 0.8 %copy-done.3 = bf16[32,1024]{1,0:T(8,128)(2,1)S(1)} copy-done((bf16[32,1024]{1,0:T(8,128)(2,1)S(1)}, bf16[32,1024]{1,0:T(8,128)(2,1)}, u32[]{:S(2)}) %copy-start.3) | copy-done | bytes 65560
  4.4 47.0 %shard_map.76 = (bf16[256,1024]{1,0:T(8,128)(2,1)S(1)}, bf16[32,1024]{1,0:T(8,128)(2,1)S(1)}, bf16[32,1024]{1,0:T(8,128)(2,1)S(1)}) custom-call(bf16[256,1024]{1,0:T(8,128)(2,1)S(1)} %copy-done, bf16[32,1024]{1,0:T(8,128)(2,1)S(1)} %copy-done.2, bf16[32,1024]{1,0:T(8,128)(2,1)S(1)} %copy-done.3, bf16[256,1024]{1,0:T(8,128)(2,1)S(1)} %copy-done.1, ...), custom_call_target="tpu_custom_call" | custom-call | tf_op jit(solution)/shard_map/pallas_call | solution.py:325
  51.4 0.8 %copy.11 = bf16[256,1024]{1,0:T(8,128)(2,1)} copy(bf16[256,1024]{1,0:T(8,128)(2,1)S(1)} %get-tuple-element.6) | data formatting | bytes 1048576
  52.2 0.6 %copy.12 = bf16[32,1024]{1,0:T(8,128)(2,1)} copy(bf16[32,1024]{1,0:T(8,128)(2,1)S(1)} %get-tuple-element.7) | data formatting | bytes 131072
  52.9 0.6 %copy.13 = bf16[32,1024]{1,0:T(8,128)(2,1)} copy(bf16[32,1024]{1,0:T(8,128)(2,1)S(1)} %get-tuple-element.8) | data formatting | bytes 131072
Async XLA Ops:
  0.6 1.0 %copy-start = (bf16[256,1024]{1,0:T(8,128)(2,1)S(1)}, bf16[256,1024]{1,0:T(8,128)(2,1)}, u32[]{:S(2)}) copy-start(bf16[256,1024]{1,0:T(8,128)(2,1)} %q_hbm.1) | copy-start | bytes 1572868
  1.7 1.0 %copy-start.1 = (bf16[256,1024]{1,0:T(8,128)(2,1)S(1)}, bf16[256,1024]{1,0:T(8,128)(2,1)}, u32[]{:S(2)}) copy-start(bf16[256,1024]{1,0:T(8,128)(2,1)} %g_hbm.1) | copy-start | bytes 1572868
  2.7 0.8 %copy-start.2 = (bf16[32,1024]{1,0:T(8,128)(2,1)S(1)}, bf16[32,1024]{1,0:T(8,128)(2,1)}, u32[]{:S(2)}) copy-start(bf16[32,1024]{1,0:T(8,128)(2,1)} %k_hbm.1) | copy-start | bytes 196612
  3.6 0.8 %copy-start.3 = (bf16[32,1024]{1,0:T(8,128)(2,1)S(1)}, bf16[32,1024]{1,0:T(8,128)(2,1)}, u32[]{:S(2)}) copy-start(bf16[32,1024]{1,0:T(8,128)(2,1)} %v_hbm.1) | copy-start | bytes 196612

commit v2 on v1

--- a/solution.py
+++ b/solution.py
@@ -35,6 +35,8 @@
     half = Z * r
     pairs = width // PAIR
     chunks = width // kc
+    group = 2 if pairs % 2 == 0 else 1
+    groups = pairs // group
     c = lax.axis_index("ctx")
     h = lax.axis_index("head")
     z, y = c // Y, c % Y
@@ -74,8 +76,55 @@
         cols = pl.ds(pl.multiple_of(block * width, width), width)
         return pltpu.make_async_copy(w_hbm.at[:, cols], wbuf.at[d, e], w_sem.at[d, e])
 
+    partners = ([at_z(b) for b in range(1, Z)] + [at_y(a) for a in range(1, Y)]
+                + [at_x(d) for d in range(1, X)] + [at_core(d) for d in range(1, C)])
+    barrier = pltpu.get_barrier_semaphore()
+    for target in partners:
+        pl.semaphore_signal(barrier, inc=1, device_id=target, device_id_type=MESH)
     loads[0].start()
     w_load(0, 0).start()
+    pl.semaphore_wait(barrier, len(partners))
+
+    def cols(j):
+        return pl.ds(j * kc, kc)
+
+    def gx(d, j):
+        return remote(g_hbm.at[:, cols(j)], gbuf.at[X - d, 0, :, cols(j)],
+                      gx_send.at[d, j], g_recv.at[X - d, 0, j], at_x(d))
+
+    def gc(e):
+        return remote(g_hbm, gbuf.at[0, C - e], gc_send.at[e], g_recv.at[0, C - e, 0], at_core(e))
+
+    def gf(d, e, j):
+        return remote(gbuf.at[d, 0, :, cols(j)], gbuf.at[d, C - e, :, cols(j)],
+                      gf_send.at[d, e, j], g_recv.at[d, C - e, j], at_core(e))
+
+    def kvz(t, b):
+        return remote(kv_hbm[t], kvbuf.at[t, slot(0, Z - b)],
+                      kvz_send.at[t, b], kv_recv.at[t, 0, Z - b], at_z(b))
+
+    def kvy(t, a):
+        return remote(kv_hbm[t], kvbuf.at[t, slot(Y - a, 0)],
+                      kvy_send.at[t, a], kv_recv.at[t, Y - a, 0], at_y(a))
+
+    def kvf(t, a, b):
+        return remote(kvbuf.at[t, slot(0, b)], kvbuf.at[t, slot(Y - a, b)],
+                      kvf_send.at[t, a, b], kv_recv.at[t, Y - a, b], at_y(a))
+
+    def start_kv(t):
+        for b in range(1, Z):
+            kvz(t, Z - b).start()
+        for a in range(1, Y):
+            kvy(t, a).start()
+
+    for d in range(1, X):
+        gx(d, 0).start()
+    start_kv(0)
+    for e in range(1, C):
+        gc(e).start()
+    for j in range(1, chunks):
+        for d in range(1, X):
+            gx(d, j).start()
     for copy in loads[1:]:
         copy.start()
     for d in range(X):
@@ -83,63 +132,23 @@
             if d + e:
                 w_load(d, e).start()
 
-    partners = ([at_z(b) for b in range(1, Z)] + [at_y(a) for a in range(1, Y)]
-                + [at_x(d) for d in range(1, X)] + [at_core(d) for d in range(1, C)])
-    barrier = pltpu.get_barrier_semaphore()
-    for target in partners:
-        pl.semaphore_signal(barrier, inc=1, device_id=target, device_id_type=MESH)
-    pl.semaphore_wait(barrier, len(partners))
-
-    def cols(j):
-        return pl.ds(j * kc, kc)
-
-    def gx(d, j):
-        return remote(g_hbm.at[:, cols(j)], gbuf.at[X - d, 0, :, cols(j)],
-                      gx_send.at[d, j], g_recv.at[X - d, 0, j], at_x(d))
-
-    def gc(e):
-        return remote(g_hbm, gbuf.at[0, C - e], gc_send.at[e], g_recv.at[0, C - e, 0], at_core(e))
-
-    def gf(d, e, j):
-        return remote(gbuf.at[d, 0, :, cols(j)], gbuf.at[d, C - e, :, cols(j)],
-                      gf_send.at[d, e, j], g_recv.at[d, C - e, j], at_core(e))
-
-    def kvz(t, b):
-        return remote(kv_hbm[t], kvbuf.at[t, slot(0, Z - b)],
-                      kvz_send.at[t, b], kv_recv.at[t, 0, Z - b], at_z(b))
-
-    def kvy(t, a):
-        return remote(kv_hbm[t], kvbuf.at[t, slot(Y - a, 0)],
-                      kvy_send.at[t, a], kv_recv.at[t, Y - a, 0], at_y(a))
-
-    def kvf(t, a, b):
-        return remote(kvbuf.at[t, slot(0, b)], kvbuf.at[t, slot(Y - a, b)],
-                      kvf_send.at[t, a, b], kv_recv.at[t, Y - a, b], at_y(a))
-
-    for d in range(1, X):
-        gx(d, 0).start()
-    for t in range(2):
-        for b in range(1, Z):
-            kvz(t, b).start()
-        for a in range(1, Y):
-            kvy(t, a).start()
-    for j in range(1, chunks):
-        for d in range(1, X):
-            gx(d, j).start()
-    for e in range(1, C):
-        gc(e).start()
-
     def forward_g(j):
         for d in range(1, X):
             gx(X - d, j).wait_recv()
             for e in range(1, C):
                 gf(d, e, j).start()
 
+    nearest = sorted(range(1, Z), key=lambda b: min(b, Z - b))
+
     def forward_kv(t):
-        for b in range(1, Z):
+        for i, b in enumerate(nearest):
             kvz(t, Z - b).wait_recv()
             for a in range(1, Y):
                 kvf(t, a, b).start()
+            if t == 0 and i == 0:
+                start_kv(1)
+        if t == 0 and not nearest:
+            start_kv(1)
 
     def arrived_kv(t):
         for a in range(1, Y):
@@ -147,13 +156,15 @@
             for b in range(1, Z):
                 kvf(t, Y - a, b).wait_recv()
 
-    def add_chunk(j):
+    def add_chunks(first, last):
+        span = slice(first * kc, last * kc)
         total = acc[...]
         for d in range(1, X):
             for e in range(C):
                 if e:
-                    gf(d, C - e, j).wait_recv()
-                total += dot(gbuf[d, e, :, j * kc:(j + 1) * kc], wbuf[d, e, :, j * kc:(j + 1) * kc], NT)
+                    for j in range(first, last):
+                        gf(d, C - e, j).wait_recv()
+                total += dot(gbuf[d, e, :, span], wbuf[d, e, :, span], NT)
         acc[...] = total
 
     loads[0].wait()
@@ -178,36 +189,43 @@
     def both_heads(block):
         return jnp.concatenate((block * low, block * high), axis=0)
 
-    def attention(p, carry):
-        q2 = both_heads(qbuf[:, at_pair(p)] * jnp.bfloat16(scale))
-        q2buf[p] = q2
-        key_pair = kvbuf[0, :, at_pair(p)]
-        ktbuf[p] = key_pair.astype(jnp.float32).T.astype(jnp.bfloat16)
-        scores = dot(key_pair, q2, NT)
-        exponent = jnp.exp(scores - jnp.max(scores, axis=0, keepdims=True))
-        pbuf[p] = exponent * (1.0 / jnp.sum(exponent, axis=0, keepdims=True))
+    def attention(g, carry):
+        members = [g * group + i for i in range(group)]
+        queries = [both_heads(qbuf[:, at_pair(p)] * jnp.bfloat16(scale)) for p in members]
+        key_pairs = [kvbuf[0, :, at_pair(p)] for p in members]
+        scores = [dot(a, b, NT) for a, b in zip(key_pairs, queries)]
+        exponents = [jnp.exp(s - jnp.max(s, axis=0, keepdims=True)) for s in scores]
+        probs = [e * (1.0 / jnp.sum(e, axis=0, keepdims=True)) for e in exponents]
+        for p, q2, key_pair, prob in zip(members, queries, key_pairs, probs):
+            q2buf[p] = q2
+            ktbuf[p] = key_pair.astype(jnp.float32).T.astype(jnp.bfloat16)
+            pbuf[p] = prob
         return carry
+
+    def attend(first, last):
+        if first < last:
+            lax.fori_loop(first, last, attention, 0)
 
     loads[1].wait()
     loads[2].wait()
+    forward_kv(0)
     forward_g(0)
-    forward_kv(0)
-    done = 0
-    for j in range(1, chunks):
-        if j == 1:
-            arrived_kv(0)
+    if chunks > 1:
+        forward_g(1)
+        add_chunks(0, 1)
+    arrived_kv(0)
+    attend(0, groups // 4)
+    if chunks > 2:
+        forward_g(2)
+    attend(groups // 4, groups // 2)
+    forward_kv(1)
+    for j in range(3, chunks):
         forward_g(j)
-        if j == min(2, chunks - 1):
-            forward_kv(1)
-        add_chunk(j - 1)
-        upto = pairs * j // (chunks - 1)
-        lax.fori_loop(done, upto, attention, 0)
-        done = upto
-    if chunks == 1:
-        arrived_kv(0)
-        forward_kv(1)
-        lax.fori_loop(0, pairs, attention, 0)
-    add_chunk(chunks - 1)
+    attend(groups // 2, 3 * groups // 4)
+    if chunks > 2:
+        add_chunks(1, chunks - 1)
+    attend(3 * groups // 4, groups)
+    add_chunks(chunks - 1, chunks)
     dobuf[...] = acc[...].astype(jnp.bfloat16)
     loads[3].wait()
     arrived_kv(1)
@@ -220,20 +238,25 @@
         return remote(s2.at[b - 1, p], r2.at[Z - b - 1, p], s2_send.at[b - 1, p],
                       r2_recv.at[Z - b - 1, p], at_z(b))
 
-    def terms(p):
-        do2 = both_heads(dobuf[:, at_pair(p)])
-        prob = pbuf[p]
-        prob_low = prob.astype(jnp.bfloat16)
-        dp = dot(kvbuf[1, :, at_pair(p)], do2, NT)
-        delta = jnp.sum(prob_low.astype(jnp.float32) * dp, axis=0, keepdims=True)
-        ds = (prob * (dp - delta)).astype(jnp.bfloat16)
-        dsbuf[p] = ds
-        for t, term in enumerate((dot(ds, q2buf[p], NN), dot(prob_low, do2, NN))):
-            part[p, t] = term[:half]
+    def terms(g):
+        members = [g * group + i for i in range(group)]
+        grads = [both_heads(dobuf[:, at_pair(p)]) for p in members]
+        dps = [dot(kvbuf[1, :, at_pair(p)], do2, NT) for p, do2 in zip(members, grads)]
+        probs = [pbuf[p] for p in members]
+        lows = [prob.astype(jnp.bfloat16) for prob in probs]
+        deltas = [jnp.sum(a.astype(jnp.float32) * b, axis=0, keepdims=True) for a, b in zip(lows, dps)]
+        scored = [(a * (b - d)).astype(jnp.bfloat16) for a, b, d in zip(probs, dps, deltas)]
+        value_terms = [dot(a, b, NN) for a, b in zip(lows, grads)]
+        key_terms = [dot(ds, q2buf[p], NN) for ds, p in zip(scored, members)]
+        for p, ds, key_term, value_term in zip(members, scored, key_terms, value_terms):
+            dsbuf[p] = ds
+            for t, term in enumerate((key_term, value_term)):
+                part[p, t] = term[:half]
+                for a in range(1, Y):
+                    s1[a - 1, p, t] = term[a * half:(a + 1) * half].astype(jnp.bfloat16)
+        for p in members:
             for a in range(1, Y):
-                s1[a - 1, p, t] = term[a * half:(a + 1) * half].astype(jnp.bfloat16)
-        for a in range(1, Y):
-            send1(a, p).start()
+                send1(a, p).start()
 
     def second(p):
         for a in range(1, Y):
@@ -253,27 +276,21 @@
         both = jnp.concatenate((dqt[:DH, :rows], dqt[DH:, rows:]), axis=0)
         dq_ref[:, at_pair(p)] = (both.T * scale).astype(jnp.bfloat16)
 
-    lag = min(2, pairs)
-
-    def first_loop(p, carry):
-        terms(p)
-
-        @pl.when(p >= lag)
+    def relay(g):
+        for i in range(group):
+            query_part(g * group + i)
+            second(g * group + i)
+
+    def first_loop(g, carry):
+        terms(g)
+
+        @pl.when(g >= 1)
         def _():
-            second(p - lag)
+            relay(g - 1)
         return carry
 
-    lax.fori_loop(0, pairs, first_loop, 0)
-
-    def tail_loop(p, carry):
-        query_part(p)
-
-        @pl.when(p >= pairs - lag)
-        def _():
-            second(p)
-        return carry
-
-    lax.fori_loop(0, pairs, tail_loop, 0)
+    lax.fori_loop(0, groups, first_loop, 0)
+    relay(groups - 1)
 
     def final_loop(p, carry):
         for b in range(1, Z):
@@ -363,7 +380,7 @@
             dma((z1, pairs)),
         ],
         compiler_params=pltpu.CompilerParams(
-            collective_id=0, has_side_effects=True, vmem_limit_bytes=52 * 1024 * 1024),
+            collective_id=0, has_side_effects=True, vmem_limit_bytes=62 * 1024 * 1024),
     )(queries, enc_keys, enc_values, grad_out, out_weight)
 
 

time: 53.8 us -> 50 us (0.929)
  Pallas kernels: 47 us -> 44.2 us
  local copies, waits for them, and re-layouts: 5.81 us -> 4.81 us
    pallas_call x1, Pallas kernels: 47 us -> 44.2 us  [local(): pl.pallas_call(functools.partial(kernel, Z, Y, X, C, kc), out_shape=(jax....]
    unnamed x11 -> x3, local copies, waits for them, and re-layouts: 5.81 us -> 4.81 us
where the time goes in v2:
time: 50 us; the launch traced here: 49.7 us
  Pallas kernels  44.2 us (88%)
  local copies, waits for them, and re-layouts  4.81 us (10%)
  between operations  0.64 us (1%)
    pallas_call x1, Pallas kernels, local(): pl.pallas_call(functools.partial(kernel, Z, Y, X, C, kc), out_shape=(jax....  44.2 us
    unnamed x3, local copies, waits for them, and re-layouts  4.81 us

profile of v2, /device:TPU:0, one launch (start us, length us, event | category | flops | bytes accessed | tf_op | source)
XLA Modules:
  0.0 49.7 jit_solution(7771319724775254866)
XLA Ops:
  0.6 44.2 %shard_map.76 = (bf16[256,1024]{1,0:T(8,128)(2,1)}, bf16[32,1024]{1,0:T(8,128)(2,1)}, bf16[32,1024]{1,0:T(8,128)(2,1)}) custom-call(bf16[256,1024]{1,0:T(8,128)(2,1)} %q_hbm.1, bf16[32,1024]{1,0:T(8,128)(2,1)} %k_hbm.1, bf16[32,1024]{1,0:T(8,128)(2,1)} %v_hbm.1, bf16[256,1024]{1,0:T(8,128)(2,1)} %g_hbm.1, bf16[1024,4096]{1,0:T(8,128)(2,1)} %w_hbm.1), custom_call_target="tpu_custom_call" | custom-call | tf_op jit(solution)/shard_map/pallas_call | solution.py:342
  44.9 1.9 %copy.11 = bf16[256,1024]{1,0:T(8,128)(2,1)} copy(bf16[256,1024]{1,0:T(8,128)(2,1)} %get-tuple-element.6) | data formatting | bytes 1048576
  46.8 1.5 %copy.12 = bf16[32,1024]{1,0:T(8,128)(2,1)} copy(bf16[32,1024]{1,0:T(8,128)(2,1)} %get-tuple-element.7) | data formatting | bytes 131072
  48.2 1.5 %copy.13 = bf16[32,1024]{1,0:T(8,128)(2,1)} copy(bf16[32,1024]{1,0:T(8,128)(2,1)} %get-tuple-element.8) | data formatting | bytes 131072

commit v3 on v2

--- a/solution.py
+++ b/solution.py
@@ -35,7 +35,7 @@
     half = Z * r
     pairs = width // PAIR
     chunks = width // kc
-    group = 2 if pairs % 2 == 0 else 1
+    group = kc // PAIR
     groups = pairs // group
     c = lax.axis_index("ctx")
     h = lax.axis_index("head")
@@ -86,7 +86,7 @@
     pl.semaphore_wait(barrier, len(partners))
 
     def cols(j):
-        return pl.ds(j * kc, kc)
+        return pl.ds(pl.multiple_of(j * kc, kc), kc)
 
     def gx(d, j):
         return remote(g_hbm.at[:, cols(j)], gbuf.at[X - d, 0, :, cols(j)],
@@ -156,24 +156,40 @@
             for b in range(1, Z):
                 kvf(t, Y - a, b).wait_recv()
 
-    def add_chunks(first, last):
-        span = slice(first * kc, last * kc)
-        total = acc[...]
+    def tiles(body):
+        def step(n, carry):
+            body(pl.ds(pl.multiple_of(n * kc, kc), kc))
+            return carry
+
+        lax.fori_loop(0, chunks, step, 0)
+
+    def add_chunk(j):
         for d in range(1, X):
-            for e in range(C):
-                if e:
-                    for j in range(first, last):
-                        gf(d, C - e, j).wait_recv()
-                total += dot(gbuf[d, e, :, span], wbuf[d, e, :, span], NT)
-        acc[...] = total
+            for e in range(1, C):
+                gf(d, C - e, j).wait_recv()
+
+        def body(tile):
+            total = acc[:, tile]
+            for d in range(1, X):
+                for e in range(C):
+                    total += dot(gbuf[d, e, :, cols(j)], wbuf[d, e, tile, cols(j)], NT)
+            acc[:, tile] = total
+
+        tiles(body)
 
     loads[0].wait()
-    w_load(0, 0).wait()
-    acc[...] = dot(gbuf[0, 0], wbuf[0, 0], NT)
-    for e in range(1, C):
-        gc(C - e).wait_recv()
+    for e in range(C):
         w_load(0, e).wait()
-        acc[...] += dot(gbuf[0, e], wbuf[0, e], NT)
+        if e:
+            gc(C - e).wait_recv()
+
+    def near_blocks(tile):
+        total = dot(gbuf[0, 0], wbuf[0, 0, tile], NT)
+        for e in range(1, C):
+            total += dot(gbuf[0, e], wbuf[0, e, tile], NT)
+        acc[:, tile] = total
+
+    tiles(near_blocks)
     for d in range(1, X):
         for e in range(C):
             w_load(d, e).wait()
@@ -189,7 +205,7 @@
     def both_heads(block):
         return jnp.concatenate((block * low, block * high), axis=0)
 
-    def attention(g, carry):
+    def attention(g):
         members = [g * group + i for i in range(group)]
         queries = [both_heads(qbuf[:, at_pair(p)] * jnp.bfloat16(scale)) for p in members]
         key_pairs = [kvbuf[0, :, at_pair(p)] for p in members]
@@ -200,32 +216,24 @@
             q2buf[p] = q2
             ktbuf[p] = key_pair.astype(jnp.float32).T.astype(jnp.bfloat16)
             pbuf[p] = prob
-        return carry
-
-    def attend(first, last):
-        if first < last:
-            lax.fori_loop(first, last, attention, 0)
 
     loads[1].wait()
     loads[2].wait()
     forward_kv(0)
-    forward_g(0)
-    if chunks > 1:
-        forward_g(1)
-        add_chunks(0, 1)
     arrived_kv(0)
-    attend(0, groups // 4)
-    if chunks > 2:
-        forward_g(2)
-    attend(groups // 4, groups // 2)
-    forward_kv(1)
-    for j in range(3, chunks):
+
+    def gather_step(j, carry):
         forward_g(j)
-    attend(groups // 2, 3 * groups // 4)
-    if chunks > 2:
-        add_chunks(1, chunks - 1)
-    attend(3 * groups // 4, groups)
-    add_chunks(chunks - 1, chunks)
+        attention(j)
+
+        @pl.when(j == min(1, chunks - 1))
+        def _():
+            forward_kv(1)
+
+        add_chunk(j)
+        return carry
+
+    lax.fori_loop(0, chunks, gather_step, 0)
     dobuf[...] = acc[...].astype(jnp.bfloat16)
     loads[3].wait()
     arrived_kv(1)
@@ -278,10 +286,9 @@
 
     def relay(g):
         for i in range(group):
-            query_part(g * group + i)
             second(g * group + i)
 
-    def first_loop(g, carry):
+    def term_step(g, carry):
         terms(g)
 
         @pl.when(g >= 1)
@@ -289,8 +296,17 @@
             relay(g - 1)
         return carry
 
-    lax.fori_loop(0, groups, first_loop, 0)
-    relay(groups - 1)
+    lax.fori_loop(0, groups, term_step, 0)
+
+    def query_step(p, carry):
+        query_part(p)
+
+        @pl.when(p == pairs // 2 - 1 if pairs > 1 else p == 0)
+        def _():
+            relay(groups - 1)
+        return carry
+
+    lax.fori_loop(0, pairs, query_step, 0)
 
     def final_loop(p, carry):
         for b in range(1, Z):
@@ -324,6 +340,15 @@
             kvy(t, a).wait_send()
 
 
+def write_results(a, b, c, a_out, b_out, c_out, sem):
+    copies = [pltpu.make_async_copy(src, dst, sem.at[i])
+              for i, (src, dst) in enumerate(((a, a_out), (b, b_out), (c, c_out)))]
+    for copy in copies:
+        copy.start()
+    for copy in copies:
+        copy.wait()
+
+
 def local(n, m, queries, enc_keys, enc_values, grad_out, out_weight):
     rows, width = queries.shape
     r = enc_keys.shape[0]
@@ -331,20 +356,20 @@
     Z = n // Y
     C = 2 if m % 2 == 0 else 1
     X = m // C
-    kc = min(256, width)
     pairs = width // PAIR
+    kc = PAIR * (2 if pairs % 2 == 0 else 1)
     chunks = width // kc
     keys, half = n * r, Z * r
     low, full = jnp.bfloat16, jnp.float32
     y1, z1 = max(Y - 1, 1), max(Z - 1, 1)
     dma = pltpu.SemaphoreType.DMA
     vmem = pltpu.VMEM
-    return pl.pallas_call(
+    results = pl.pallas_call(
         functools.partial(kernel, Z, Y, X, C, kc),
         out_shape=(
-            jax.ShapeDtypeStruct((rows, width), low),
-            jax.ShapeDtypeStruct((r, width), low),
-            jax.ShapeDtypeStruct((r, width), low),
+            pltpu.VMEM((rows, width), low),
+            pltpu.VMEM((r, width), low),
+            pltpu.VMEM((r, width), low),
         ),
         in_specs=[pl.BlockSpec(memory_space=pl.ANY)] * 5,
         out_specs=[pl.BlockSpec(memory_space=pltpu.VMEM)] * 3,
@@ -382,6 +407,13 @@
         compiler_params=pltpu.CompilerParams(
             collective_id=0, has_side_effects=True, vmem_limit_bytes=62 * 1024 * 1024),
     )(queries, enc_keys, enc_values, grad_out, out_weight)
+    return pl.pallas_call(
+        write_results,
+        out_shape=tuple(jax.ShapeDtypeStruct(a.shape, a.dtype) for a in results),
+        in_specs=[pl.BlockSpec(memory_space=pl.ANY)] * 3,
+        out_specs=[pl.BlockSpec(memory_space=pl.ANY)] * 3,
+        scratch_shapes=[dma((3,))],
+    )(*results)
 
 
 def solution(mesh):

time: 50 us -> 71.6 us (1.43)
  Pallas kernels: 44.2 us -> 68.8 us
  local copies, waits for them, and re-layouts: 4.81 us -> 2.02 us
    pallas_call x1 -> x2, Pallas kernels: 44.2 us -> 68.8 us  [the longest x1 47.8 us: local(): pl.pallas_call(functools.partial(kernel, Z, Y, X, C, kc), out_shape=(pltp...]
    unnamed x3 -> x6, local copies, waits for them, and re-layouts: 4.81 us -> 2.02 us
where the time goes in v3:
time: 71.6 us; the launch traced here: 71.4 us
  Pallas kernels  68.8 us (96%)
  local copies, waits for them, and re-layouts  2.02 us (3%)
    pallas_call x1, Pallas kernels, local(): pl.pallas_call(functools.partial(kernel, Z, Y, X, C, kc), out_shape=(pltp...  47.8 us
    pallas_call x1, Pallas kernels, local(): pl.pallas_call(write_results, out_shape=tuple((jax.ShapeDtypeStruct(a.sha...  21 us
    unnamed x6, local copies, waits for them, and re-layouts  2.02 us

profile of v3, /device:TPU:0, one launch (start us, length us, event | category | flops | bytes accessed | tf_op | source)
XLA Modules:
  0.0 71.4 jit_solution(15102051600707012827)
XLA Ops:
  0.6 47.8 %shard_map.76 = (bf16[256,1024]{1,0:T(8,128)(2,1)S(1)}, bf16[32,1024]{1,0:T(8,128)(2,1)S(1)}, bf16[32,1024]{1,0:T(8,128)(2,1)S(1)}) custom-call(bf16[256,1024]{1,0:T(8,128)(2,1)} %q_hbm.1, bf16[32,1024]{1,0:T(8,128)(2,1)} %k_hbm.1, bf16[32,1024]{1,0:T(8,128)(2,1)} %v_hbm.1, bf16[256,1024]{1,0:T(8,128)(2,1)} %g_hbm.1, bf16[1024,4096]{1,0:T(8,128)(2,1)} %w_hbm.1), custom_call_target="tpu_custom_call" | custom-call | tf_op jit(solution)/shard_map/pallas_call | solution.py:367
  48.4 0.0 copy-start
  48.5 0.8 %copy-done = bf16[256,1024]{1,0:T(8,128)(2,1)} copy-done((bf16[256,1024]{1,0:T(8,128)(2,1)}, bf16[256,1024]{1,0:T(8,128)(2,1)S(1)}, u32[]{:S(2)}) %copy-start) | copy-done | bytes 524312
  49.2 0.0 copy-start.1
  49.2 0.6 copy-done.1
  49.8 0.0 copy-start.2
  49.9 0.6 copy-done.2
  50.5 21.0 %shard_map.77 = (bf16[256,1024]{1,0:T(8,128)(2,1)}, bf16[32,1024]{1,0:T(8,128)(2,1)}, bf16[32,1024]{1,0:T(8,128)(2,1)}) custom-call(bf16[256,1024]{1,0:T(8,128)(2,1)} %copy-done, bf16[32,1024]{1,0:T(8,128)(2,1)} %copy-done.1, bf16[32,1024]{1,0:T(8,128)(2,1)} %copy-done.2), custom_call_target="tpu_custom_call" | custom-call | tf_op jit(solution)/shard_map/pallas_call | solution.py:410
Async XLA Ops:
  48.4 0.8 %copy-start = (bf16[256,1024]{1,0:T(8,128)(2,1)}, bf16[256,1024]{1,0:T(8,128)(2,1)S(1)}, u32[]{:S(2)}) copy-start(bf16[256,1024]{1,0:T(8,128)(2,1)S(1)} %get-tuple-element.6.a) | copy-start | bytes 1572868
  49.2 0.6 copy-start.1
  49.8 0.6 copy-start.2

commit v4 on v2

--- a/solution.py
+++ b/solution.py
@@ -62,8 +62,6 @@
     def slot(a, b):
         return pl.ds((a * Z + b) * r, r)
 
-    kv_hbm = (k_hbm, v_hbm)
-
     loads = [
         pltpu.make_async_copy(g_hbm, gbuf.at[0, 0], loc_sem.at[0]),
         pltpu.make_async_copy(q_hbm, qbuf, loc_sem.at[1]),
@@ -81,7 +79,8 @@
     barrier = pltpu.get_barrier_semaphore()
     for target in partners:
         pl.semaphore_signal(barrier, inc=1, device_id=target, device_id_type=MESH)
-    loads[0].start()
+    for i in (0, 2, 3):
+        loads[i].start()
     w_load(0, 0).start()
     pl.semaphore_wait(barrier, len(partners))
 
@@ -89,22 +88,22 @@
         return pl.ds(j * kc, kc)
 
     def gx(d, j):
-        return remote(g_hbm.at[:, cols(j)], gbuf.at[X - d, 0, :, cols(j)],
+        return remote(gbuf.at[0, 0, :, cols(j)], gbuf.at[X - d, 0, :, cols(j)],
                       gx_send.at[d, j], g_recv.at[X - d, 0, j], at_x(d))
 
     def gc(e):
-        return remote(g_hbm, gbuf.at[0, C - e], gc_send.at[e], g_recv.at[0, C - e, 0], at_core(e))
+        return remote(gbuf.at[0, 0], gbuf.at[0, C - e], gc_send.at[e], g_recv.at[0, C - e, 0], at_core(e))
 
     def gf(d, e, j):
         return remote(gbuf.at[d, 0, :, cols(j)], gbuf.at[d, C - e, :, cols(j)],
                       gf_send.at[d, e, j], g_recv.at[d, C - e, j], at_core(e))
 
     def kvz(t, b):
-        return remote(kv_hbm[t], kvbuf.at[t, slot(0, Z - b)],
+        return remote(kvbuf.at[t, slot(0, 0)], kvbuf.at[t, slot(0, Z - b)],
                       kvz_send.at[t, b], kv_recv.at[t, 0, Z - b], at_z(b))
 
     def kvy(t, a):
-        return remote(kv_hbm[t], kvbuf.at[t, slot(Y - a, 0)],
+        return remote(kvbuf.at[t, slot(0, 0)], kvbuf.at[t, slot(Y - a, 0)],
                       kvy_send.at[t, a], kv_recv.at[t, Y - a, 0], at_y(a))
 
     def kvf(t, a, b):
@@ -117,16 +116,18 @@
         for a in range(1, Y):
             kvy(t, a).start()
 
+    loads[0].wait()
     for d in range(1, X):
         gx(d, 0).start()
+    loads[2].wait()
     start_kv(0)
     for e in range(1, C):
         gc(e).start()
     for j in range(1, chunks):
         for d in range(1, X):
             gx(d, j).start()
-    for copy in loads[1:]:
-        copy.start()
+    loads[3].wait()
+    loads[1].start()
     for d in range(X):
         for e in range(C):
             if d + e:
@@ -164,24 +165,28 @@
                 if e:
                     for j in range(first, last):
                         gf(d, C - e, j).wait_recv()
-                total += dot(gbuf[d, e, :, span], wbuf[d, e, :, span], NT)
+                total += dot(wbuf[d, e, :, span], gbuf[d, e, :, span], NT)
         acc[...] = total
 
-    loads[0].wait()
-    w_load(0, 0).wait()
-    acc[...] = dot(gbuf[0, 0], wbuf[0, 0], NT)
-    for e in range(1, C):
-        gc(C - e).wait_recv()
-        w_load(0, e).wait()
-        acc[...] += dot(gbuf[0, e], wbuf[0, e], NT)
-    for d in range(1, X):
-        for e in range(C):
-            w_load(d, e).wait()
+    def near_blocks():
+        w_load(0, 0).wait()
+        total = dot(wbuf[0, 0], gbuf[0, 0], NT)
+        for e in range(1, C):
+            gc(C - e).wait_recv()
+            w_load(0, e).wait()
+            total += dot(wbuf[0, e], gbuf[0, e], NT)
+        acc[...] = total
+        for d in range(1, X):
+            for e in range(C):
+                w_load(d, e).wait()
 
     lane = lax.broadcasted_iota(jnp.int32, (1, PAIR), 1)
     low = jnp.where(lane < DH, 1.0, 0.0).astype(jnp.bfloat16)
     high = jnp.where(lane < DH, 0.0, 1.0).astype(jnp.bfloat16)
     scale = DH ** -0.5
+    row = lax.broadcasted_iota(jnp.int32, (PAIR, 1), 0)
+    upper = jnp.where(row < DH, 1.0, 0.0).astype(jnp.bfloat16)
+    lower = jnp.where(row < DH, 0.0, 1.0).astype(jnp.bfloat16)
 
     def at_pair(p):
         return pl.ds(pl.multiple_of(p * PAIR, PAIR), PAIR)
@@ -206,13 +211,12 @@
         if first < last:
             lax.fori_loop(first, last, attention, 0)
 
-    loads[1].wait()
-    loads[2].wait()
     forward_kv(0)
     forward_g(0)
+    near_blocks()
     if chunks > 1:
         forward_g(1)
-        add_chunks(0, 1)
+    loads[1].wait()
     arrived_kv(0)
     attend(0, groups // 4)
     if chunks > 2:
@@ -221,32 +225,31 @@
     forward_kv(1)
     for j in range(3, chunks):
         forward_g(j)
-    attend(groups // 2, 3 * groups // 4)
-    if chunks > 2:
-        add_chunks(1, chunks - 1)
-    attend(3 * groups // 4, groups)
-    add_chunks(chunks - 1, chunks)
+    add_chunks(0, (chunks + 1) // 2)
+    attend(groups // 2, groups)
+    if chunks > 1:
+        add_chunks((chunks + 1) // 2, chunks)
     dobuf[...] = acc[...].astype(jnp.bfloat16)
-    loads[3].wait()
     arrived_kv(1)
 
     def send1(a, p):
-        return remote(s1.at[a - 1, p], r1.at[Y - a - 1, p], s1_send.at[a - 1, p],
+        return remote(s1.at[a - 1, p], r1.at[Y - a - 1, p], s1_send.at[a - 1],
                       r1_recv.at[Y - a - 1, p], at_y(a))
 
     def send2(b, p):
-        return remote(s2.at[b - 1, p], r2.at[Z - b - 1, p], s2_send.at[b - 1, p],
-                      r2_recv.at[Z - b - 1, p], at_z(b))
+        return remote(s2.at[b - 1, p], r2.at[Z - b - 1, p], s2_send.at[b - 1],
+                      r2_recv.at[Z - b - 1], at_z(b))
 
     def terms(g):
         members = [g * group + i for i in range(group)]
-        grads = [both_heads(dobuf[:, at_pair(p)]) for p in members]
-        dps = [dot(kvbuf[1, :, at_pair(p)], do2, NT) for p, do2 in zip(members, grads)]
+        blocks = [dobuf[at_pair(p)] for p in members]
+        grads = [jnp.concatenate((block * upper, block * lower), axis=1) for block in blocks]
+        dps = [dot(kvbuf[1, :, at_pair(p)], do2, NN) for p, do2 in zip(members, grads)]
         probs = [pbuf[p] for p in members]
         lows = [prob.astype(jnp.bfloat16) for prob in probs]
         deltas = [jnp.sum(a.astype(jnp.float32) * b, axis=0, keepdims=True) for a, b in zip(lows, dps)]
         scored = [(a * (b - d)).astype(jnp.bfloat16) for a, b, d in zip(probs, dps, deltas)]
-        value_terms = [dot(a, b, NN) for a, b in zip(lows, grads)]
+        value_terms = [dot(a, b, NT) for a, b in zip(lows, grads)]
         key_terms = [dot(ds, q2buf[p], NN) for ds, p in zip(scored, members)]
         for p, ds, key_term, value_term in zip(members, scored, key_terms, value_terms):
             dsbuf[p] = ds
@@ -292,21 +295,25 @@
     lax.fori_loop(0, groups, first_loop, 0)
     relay(groups - 1)
 
-    def final_loop(p, carry):
-        for b in range(1, Z):
-            send2(Z - b, p).wait_recv()
+    def all1(a):
+        return remote(s1.at[a - 1], r1.at[Y - a - 1], s1_send.at[a - 1], r1_recv.at[Y - a - 1, 0], at_y(a))
+
+    def all2(b):
+        return remote(s2.at[b - 1], r2.at[Z - b - 1], s2_send.at[b - 1], r2_recv.at[Z - b - 1], at_z(b))
+
+    for b in range(1, Z):
+        all2(Z - b).wait_recv()
+
+    for p in range(pairs):
         for t, out in enumerate((dk_ref, dv_ref)):
             total = part[p, t, :r]
             for b in range(1, Z):
                 total += r2[b - 1, p, t].astype(jnp.float32)
-            out[:, at_pair(p)] = total.astype(jnp.bfloat16)
-        for a in range(1, Y):
-            send1(a, p).wait_send()
-        for b in range(1, Z):
-            send2(b, p).wait_send()
-        return carry
-
-    lax.fori_loop(0, pairs, final_loop, 0)
+            out[:, p * PAIR:(p + 1) * PAIR] = total.astype(jnp.bfloat16)
+    for a in range(1, Y):
+        all1(a).wait_send()
+    for b in range(1, Z):
+        all2(b).wait_send()
 
     for j in range(chunks):
         for d in range(1, X):
@@ -342,9 +349,9 @@
     return pl.pallas_call(
         functools.partial(kernel, Z, Y, X, C, kc),
         out_shape=(
-            jax.ShapeDtypeStruct((rows, width), low),
-            jax.ShapeDtypeStruct((r, width), low),
-            jax.ShapeDtypeStruct((r, width), low),
+            pltpu.VMEM((rows, width), low),
+            pltpu.VMEM((r, width), low),
+            pltpu.VMEM((r, width), low),
         ),
         in_specs=[pl.BlockSpec(memory_space=pl.ANY)] * 5,
         out_specs=[pl.BlockSpec(memory_space=pltpu.VMEM)] * 3,
@@ -355,8 +362,8 @@
             vmem((pairs, PAIR, keys), low),
             vmem((X, C, rows, width), low),
             vmem((X, C, width, width), low),
-            vmem((rows, width), full),
-            vmem((rows, width), low),
+            vmem((width, rows), full),
+            vmem((width, rows), low),
             vmem((pairs, keys, 2 * rows), full),
             vmem((pairs, keys, 2 * rows), low),
             vmem((pairs, 2, half, PAIR), full),
@@ -374,10 +381,10 @@
             dma((2, Z)),
             dma((2, Y)),
             dma((2, Y, Z)),
+            dma((y1,)),
             dma((y1, pairs)),
-            dma((y1, pairs)),
-            dma((z1, pairs)),
-            dma((z1, pairs)),
+            dma((z1,)),
+            dma((z1,)),
         ],
         compiler_params=pltpu.CompilerParams(
             collective_id=0, has_side_effects=True, vmem_limit_bytes=62 * 1024 * 1024),

time: 50 us -> 46.9 us (0.938)
  local copies, waits for them, and re-layouts: 4.81 us -> 2.05 us
    unnamed x3, local copies, waits for them, and re-layouts: 4.81 us -> 2.05 us
where the time goes in v4:
time: 46.9 us; the launch traced here: 46.7 us
  Pallas kernels  44.1 us (94%)
  local copies, waits for them, and re-layouts  2.05 us (4%)
  between operations  0.64 us (1%)
    pallas_call x1, Pallas kernels, local(): pl.pallas_call(functools.partial(kernel, Z, Y, X, C, kc), out_shape=(pltp...  44.1 us
    unnamed x3, local copies, waits for them, and re-layouts  2.05 us

profile of v4, /device:TPU:0, one launch (start us, length us, event | category | flops | bytes accessed | tf_op | source)
XLA Modules:
  0.0 46.7 jit_solution(10946152311377085244)
XLA Ops:
  0.6 44.1 %shard_map.76 = (bf16[256,1024]{1,0:T(8,128)(2,1)S(1)}, bf16[32,1024]{1,0:T(8,128)(2,1)S(1)}, bf16[32,1024]{1,0:T(8,128)(2,1)S(1)}) custom-call(bf16[256,1024]{1,0:T(8,128)(2,1)} %q_hbm.1, bf16[32,1024]{1,0:T(8,128)(2,1)} %k_hbm.1, bf16[32,1024]{1,0:T(8,128)(2,1)} %v_hbm.1, bf16[256,1024]{1,0:T(8,128)(2,1)} %g_hbm.1, bf16[1024,4096]{1,0:T(8,128)(2,1)} %w_hbm.1), custom_call_target="tpu_custom_call" | custom-call | tf_op jit(solution)/shard_map/pallas_call | solution.py:349
  44.7 0.8 %copy.11 = bf16[256,1024]{1,0:T(8,128)(2,1)} copy(bf16[256,1024]{1,0:T(8,128)(2,1)S(1)} %get-tuple-element.3) | data formatting | bytes 1048576
  45.5 0.6 %copy.12 = bf16[32,1024]{1,0:T(8,128)(2,1)} copy(bf16[32,1024]{1,0:T(8,128)(2,1)S(1)} %get-tuple-element.4) | data formatting | bytes 131072
  46.1 0.6 %copy.13 = bf16[32,1024]{1,0:T(8,128)(2,1)} copy(bf16[32,1024]{1,0:T(8,128)(2,1)S(1)} %get-tuple-element.5) | data formatting | bytes 131072

commit v5 on v4

--- a/solution.py
+++ b/solution.py
@@ -98,9 +98,19 @@
         return remote(gbuf.at[d, 0, :, cols(j)], gbuf.at[d, C - e, :, cols(j)],
                       gf_send.at[d, e, j], g_recv.at[d, C - e, j], at_core(e))
 
-    def kvz(t, b):
-        return remote(kvbuf.at[t, slot(0, 0)], kvbuf.at[t, slot(0, Z - b)],
-                      kvz_send.at[t, b], kv_recv.at[t, 0, Z - b], at_z(b))
+    def kv_up(t, i):
+        return remote(kvbuf.at[t, slot(0, (Z - i) % Z)], kvbuf.at[t, slot(0, Z - i - 1)],
+                      kvz_send.at[t, 0, i], kv_recv.at[t, 0, Z - i - 1], at_z(1))
+
+    def kv_down(t, i):
+        return remote(kvbuf.at[t, slot(0, i)], kvbuf.at[t, slot(0, i + 1)],
+                      kvz_send.at[t, 1, i], kv_recv.at[t, 0, i + 1], at_z(Z - 1))
+
+    def goes_up(i):
+        return jnp.logical_and(z >= i, z < Z - 1)
+
+    def goes_down(i):
+        return jnp.logical_and(z + i <= Z - 1, z > 0)
 
     def kvy(t, a):
         return remote(kvbuf.at[t, slot(0, 0)], kvbuf.at[t, slot(Y - a, 0)],
@@ -111,8 +121,9 @@
                       kvf_send.at[t, a, b], kv_recv.at[t, Y - a, b], at_y(a))
 
     def start_kv(t):
-        for b in range(1, Z):
-            kvz(t, Z - b).start()
+        if Z > 1:
+            pl.when(goes_up(0))(lambda: kv_up(t, 0).start())
+            pl.when(goes_down(0))(lambda: kv_down(t, 0).start())
         for a in range(1, Y):
             kvy(t, a).start()
 
@@ -121,12 +132,13 @@
         gx(d, 0).start()
     loads[2].wait()
     start_kv(0)
+    loads[3].wait()
+    start_kv(1)
     for e in range(1, C):
         gc(e).start()
     for j in range(1, chunks):
         for d in range(1, X):
             gx(d, j).start()
-    loads[3].wait()
     loads[1].start()
     for d in range(X):
         for e in range(C):
@@ -139,17 +151,25 @@
             for e in range(1, C):
                 gf(d, e, j).start()
 
-    nearest = sorted(range(1, Z), key=lambda b: min(b, Z - b))
-
-    def forward_kv(t):
-        for i, b in enumerate(nearest):
-            kvz(t, Z - b).wait_recv()
+    def relay_kv(t, i):
+        if i > Z - 1:
+            return
+
+        @pl.when(z >= i)
+        def _():
+            kv_up(t, i - 1).wait_recv()
+            if i < Z - 1:
+                pl.when(z < Z - 1)(lambda: kv_up(t, i).start())
             for a in range(1, Y):
-                kvf(t, a, b).start()
-            if t == 0 and i == 0:
-                start_kv(1)
-        if t == 0 and not nearest:
-            start_kv(1)
+                kvf(t, a, Z - i).start()
+
+        @pl.when(z + i <= Z - 1)
+        def _():
+            kv_down(t, i - 1).wait_recv()
+            if i < Z - 1:
+                pl.when(z > 0)(lambda: kv_down(t, i).start())
+            for a in range(1, Y):
+                kvf(t, a, i).start()
 
     def arrived_kv(t):
         for a in range(1, Y):
@@ -168,14 +188,15 @@
                 total += dot(wbuf[d, e, :, span], gbuf[d, e, :, span], NT)
         acc[...] = total
 
-    def near_blocks():
+    def own_block():
         w_load(0, 0).wait()
-        total = dot(wbuf[0, 0], gbuf[0, 0], NT)
+        acc[...] = dot(wbuf[0, 0], gbuf[0, 0], NT)
+
+    def core_blocks():
         for e in range(1, C):
             gc(C - e).wait_recv()
             w_load(0, e).wait()
-            total += dot(wbuf[0, e], gbuf[0, e], NT)
-        acc[...] = total
+            acc[...] += dot(wbuf[0, e], gbuf[0, e], NT)
         for d in range(1, X):
             for e in range(C):
                 w_load(d, e).wait()
@@ -211,24 +232,32 @@
         if first < last:
             lax.fori_loop(first, last, attention, 0)
 
-    forward_kv(0)
+    mid = (chunks + 1) // 2
+    own_block()
+    relay_kv(0, 1)
+    relay_kv(1, 1)
+    core_blocks()
+    relay_kv(0, 2)
     forward_g(0)
-    near_blocks()
-    if chunks > 1:
-        forward_g(1)
+    relay_kv(1, 2)
+    for i in range(3, Z):
+        relay_kv(0, i)
+    for j in range(1, mid):
+        forward_g(j)
+    add_chunks(0, mid)
+    for i in range(3, Z):
+        relay_kv(1, i)
     loads[1].wait()
     arrived_kv(0)
-    attend(0, groups // 4)
-    if chunks > 2:
-        forward_g(2)
-    attend(groups // 4, groups // 2)
-    forward_kv(1)
-    for j in range(3, chunks):
+    attend(0, groups // 2)
+    for j in range(mid, chunks - 1):
         forward_g(j)
-    add_chunks(0, (chunks + 1) // 2)
     attend(groups // 2, groups)
     if chunks > 1:
-        add_chunks((chunks + 1) // 2, chunks)
+        forward_g(chunks - 1)
+        if mid < chunks - 1:
+            add_chunks(mid, chunks - 1)
+        add_chunks(chunks - 1, chunks)
     dobuf[...] = acc[...].astype(jnp.bfloat16)
     arrived_kv(1)
 
@@ -323,8 +352,10 @@
     for e in range(1, C):
         gc(e).wait_send()
     for t in range(2):
+        for i in range(Z - 1):
+            pl.when(goes_up(i))(lambda: kv_up(t, i).wait_send())
+            pl.when(goes_down(i))(lambda: kv_down(t, i).wait_send())
         for b in range(1, Z):
-            kvz(t, b).wait_send()
             for a in range(1, Y):
                 kvf(t, a, b).wait_send()
         for a in range(1, Y):
@@ -378,7 +409,7 @@
             dma((C,)),
             dma((X, C, chunks)),
             dma((2, Y, Z)),
-            dma((2, Z)),
+            dma((2, 2, Z)),
             dma((2, Y)),
             dma((2, Y, Z)),
             dma((y1,)),

time: 46.9 us -> 44.3 us (0.945)
  Pallas kernels: 44.1 us -> 41.4 us
    pallas_call x1, Pallas kernels: 44.1 us -> 41.4 us  [local(): pl.pallas_call(functools.partial(kernel, Z, Y, X, C, kc), out_shape=(pltp...]
where the time goes in v5:
time: 44.3 us; the launch traced here: 44.1 us
  Pallas kernels  41.4 us (93%)
  local copies, waits for them, and re-layouts  2.05 us (5%)
  between operations  0.64 us (1%)
    pallas_call x1, Pallas kernels, local(): pl.pallas_call(functools.partial(kernel, Z, Y, X, C, kc), out_shape=(pltp...  41.4 us
    unnamed x3, local copies, waits for them, and re-layouts  2.05 us

profile of v5, /device:TPU:0, one launch (start us, length us, event | category | flops | bytes accessed | tf_op | source)
XLA Modules:
  0.0 44.1 jit_solution(8135517615950936641)
XLA Ops:
  0.6 41.4 %shard_map.76 = (bf16[256,1024]{1,0:T(8,128)(2,1)S(1)}, bf16[32,1024]{1,0:T(8,128)(2,1)S(1)}, bf16[32,1024]{1,0:T(8,128)(2,1)S(1)}) custom-call(bf16[256,1024]{1,0:T(8,128)(2,1)} %q_hbm.1, bf16[32,1024]{1,0:T(8,128)(2,1)} %k_hbm.1, bf16[32,1024]{1,0:T(8,128)(2,1)} %v_hbm.1, bf16[256,1024]{1,0:T(8,128)(2,1)} %g_hbm.1, bf16[1024,4096]{1,0:T(8,128)(2,1)} %w_hbm.1), custom_call_target="tpu_custom_call" | custom-call | tf_op jit(solution)/shard_map/pallas_call | solution.py:380
  42.1 0.8 %copy.11 = bf16[256,1024]{1,0:T(8,128)(2,1)} copy(bf16[256,1024]{1,0:T(8,128)(2,1)S(1)} %get-tuple-element.3) | data formatting | bytes 1048576
  42.9 0.6 %copy.12 = bf16[32,1024]{1,0:T(8,128)(2,1)} copy(bf16[32,1024]{1,0:T(8,128)(2,1)S(1)} %get-tuple-element.4) | data formatting | bytes 131072
  43.5 0.6 %copy.13 = bf16[32,1024]{1,0:T(8,128)(2,1)} copy(bf16[32,1024]{1,0:T(8,128)(2,1)S(1)} %get-tuple-element.5) | data formatting | bytes 131072

commit v6 on v5

--- a/solution.py
+++ b/solution.py
@@ -26,7 +26,7 @@
 
 
 def kernel(Z, Y, X, C, kc, q_hbm, k_hbm, v_hbm, g_hbm, w_hbm, dq_ref, dk_ref, dv_ref,
-           qbuf, q2buf, kvbuf, ktbuf, gbuf, wbuf, acc, dobuf, pbuf, dsbuf, part, s1, r1, s2, r2,
+           qbuf, q2buf, kvbuf, ktbuf, gbuf, wbuf, acc, pbuf, dsbuf, part, s1, r1, s2, r2,
            loc_sem, w_sem, g_recv, gx_send, gc_send, gf_send, kv_recv, kvz_send, kvy_send, kvf_send,
            s1_send, r1_recv, s2_send, r2_recv):
     rows, width = q_hbm.shape
@@ -255,11 +255,11 @@
     attend(groups // 2, groups)
     if chunks > 1:
         forward_g(chunks - 1)
-        if mid < chunks - 1:
-            add_chunks(mid, chunks - 1)
-        add_chunks(chunks - 1, chunks)
-    dobuf[...] = acc[...].astype(jnp.bfloat16)
     arrived_kv(1)
+    for d in range(1, X):
+        for e in range(1, C):
+            for j in range(mid, chunks):
+                gf(d, C - e, j).wait_recv()
 
     def send1(a, p):
         return remote(s1.at[a - 1, p], r1.at[Y - a - 1, p], s1_send.at[a - 1],
@@ -271,7 +271,15 @@
 
     def terms(g):
         members = [g * group + i for i in range(group)]
-        blocks = [dobuf[at_pair(p)] for p in members]
+        inner = pl.ds(pl.multiple_of(g * kc, kc), kc)
+        total = acc[inner]
+        if mid < chunks:
+            span = slice(mid * kc, chunks * kc)
+            for d in range(1, X):
+                for e in range(C):
+                    total += dot(wbuf[d, e, inner, span], gbuf[d, e, :, span], NT)
+        head_grads = total.astype(jnp.bfloat16)
+        blocks = [head_grads[i * PAIR:(i + 1) * PAIR] for i in range(group)]
         grads = [jnp.concatenate((block * upper, block * lower), axis=1) for block in blocks]
         dps = [dot(kvbuf[1, :, at_pair(p)], do2, NN) for p, do2 in zip(members, grads)]
         probs = [pbuf[p] for p in members]
@@ -394,7 +402,6 @@
             vmem((X, C, rows, width), low),
             vmem((X, C, width, width), low),
             vmem((width, rows), full),
-            vmem((width, rows), low),
             vmem((pairs, keys, 2 * rows), full),
             vmem((pairs, keys, 2 * rows), low),
             vmem((pairs, 2, half, PAIR), full),

time: 44.3 us -> 44.3 us (level)
  no operation moved by 1% of the time
where the time goes in v6:
time: 44.3 us; the launch traced here: 44.1 us
  Pallas kernels  41.4 us (93%)
  local copies, waits for them, and re-layouts  2.05 us (5%)
  between operations  0.64 us (1%)
    pallas_call x1, Pallas kernels, local(): pl.pallas_call(functools.partial(kernel, Z, Y, X, C, kc), out_shape=(pltp...  41.4 us
    unnamed x3, local copies, waits for them, and re-layouts  2.05 us

profile of v6, /device:TPU:0, one launch (start us, length us, event | category | flops | bytes accessed | tf_op | source)
XLA Modules:
  0.0 44.1 jit_solution(5826703661354387784)
XLA Ops:
  0.6 41.4 %shard_map.76 = (bf16[256,1024]{1,0:T(8,128)(2,1)S(1)}, bf16[32,1024]{1,0:T(8,128)(2,1)S(1)}, bf16[32,1024]{1,0:T(8,128)(2,1)S(1)}) custom-call(bf16[256,1024]{1,0:T(8,128)(2,1)} %q_hbm.1, bf16[32,1024]{1,0:T(8,128)(2,1)} %k_hbm.1, bf16[32,1024]{1,0:T(8,128)(2,1)} %v_hbm.1, bf16[256,1024]{1,0:T(8,128)(2,1)} %g_hbm.1, bf16[1024,4096]{1,0:T(8,128)(2,1)} %w_hbm.1), custom_call_target="tpu_custom_call" | custom-call | tf_op jit(solution)/shard_map/pallas_call | solution.py:388
  42.1 0.8 %copy.11 = bf16[256,1024]{1,0:T(8,128)(2,1)} copy(bf16[256,1024]{1,0:T(8,128)(2,1)S(1)} %get-tuple-element.3) | data formatting | bytes 1048576
  42.9 0.6 %copy.12 = bf16[32,1024]{1,0:T(8,128)(2,1)} copy(bf16[32,1024]{1,0:T(8,128)(2,1)S(1)} %get-tuple-element.4) | data formatting | bytes 131072
  43.5 0.6 %copy.13 = bf16[32,1024]{1,0:T(8,128)(2,1)} copy(bf16[32,1024]{1,0:T(8,128)(2,1)S(1)} %get-tuple-element.5) | data formatting | bytes 131072
